TPU v7x, 512 devices: a whole 4x8x8 slice. The times are simulated.
512 devices in a mesh: dp: 64 (over y_lo, x, z), space: 8 (over y_hi, core).
Axes of the slice: x: 4, y: 8 (y_hi: 4, y_lo: 2; y = y_hi * 2 + y_lo), z: 8, core: 2. Of those that a mesh axis runs over, the one named last changes fastest.
Arguments:
- field_in: bfloat16 [1, 512, 512, 128], P(None, 'space', 'dp'), may hold values from -6 to 6
- pre_act: bfloat16 [1, 512, 512, 128], P(None, 'space', 'dp'), may hold values from -8 to 8
- cotangent: bfloat16 [1, 512, 512, 128], P(None, 'space', 'dp'), may hold values from -6 to 6
- spec_weight: bfloat16 [64, 64, 2, 128, 128], P('dp', 'space'), may hold values from -0.25 to 0.25
- local_weight: bfloat16 [128, 128], replicated, may hold values from -0.5 to 0.5
Outputs:
- grad_input: bfloat16 [1, 512, 512, 128], P(None, 'space', 'dp')
- grad_spectral: bfloat16 [64, 64, 2, 128, 128], P('dp', 'space')
- grad_local: float32 [128, 128], replicated
- grad_bias: float32 [128], replicated
All inputs are finite; a program needn't handle non-finite values.
Results may differ from a plain program's by a relative error of at most 0.0075.
The roundings to bfloat16 on the way count: a program that leaves them out, or rounds other values in their place, can miss the bound.
Values may be sent and summed in bfloat16 or wider, within the bound.
A program may use at most 64 MiB of HBM per device.

v0:
```python
import math
import jax
import jax.numpy as jnp
from jax import lax
from jax.sharding import PartitionSpec as P

root_two_pi = 0.7978845608028654
cubic_coef = 0.044715


def gelu_slope(values):
    tangent = jnp.tanh(root_two_pi * (values + cubic_coef * values * values * values))
    return 0.5 * (1.0 + tangent) + 0.5 * values * (1.0 - tangent * tangent) * root_two_pi * (
        1.0 + 3.0 * cubic_coef * values * values
    )


def y_basis(grid_cols, ky_count):
    positions = jnp.arange(grid_cols, dtype=jnp.int32)
    frequency = jnp.arange(ky_count, dtype=jnp.int32)
    phases = positions[:, None] * frequency[None, :] % grid_cols
    angles = phases.astype(jnp.float32) * (2.0 * math.pi / grid_cols)
    basis_table = jnp.stack([jnp.cos(angles), -jnp.sin(angles)], axis=2).reshape(
        grid_cols, 2 * ky_count
    )
    return basis_table.astype(jnp.bfloat16)


def x_rows_table(positions, grid_rows, kx_count):
    mode_index = jnp.arange(kx_count, dtype=jnp.int32)
    frequency = jnp.where(mode_index < kx_count // 2, mode_index, mode_index - kx_count)
    phases = frequency[:, None] * positions[None, :] % grid_rows
    angles = phases.astype(jnp.float32) * (2.0 * math.pi / grid_rows)
    cosine = jnp.cos(angles)
    sine = jnp.sin(angles)
    upper_rows = jnp.stack([cosine, sine], axis=1)
    lower_rows = jnp.stack([-sine, cosine], axis=1)
    return jnp.stack([upper_rows, lower_rows], axis=0).astype(jnp.bfloat16)


def on_device(field_in, pre_act, cotangent, spec_weight, local_weight):
    batch_size, slab_rows, col_block, channels = field_in.shape
    space_count = lax.axis_size("space")
    data_count = lax.axis_size("dp")
    grid_rows = slab_rows * space_count
    grid_cols = col_block * data_count
    row_count = slab_rows // data_count
    held_count = space_count * row_count
    kx_local = spec_weight.shape[0]
    kx_count = kx_local * data_count
    ky_local = spec_weight.shape[1]
    ky_count = ky_local * space_count
    data_index = lax.axis_index("dp")
    space_index = lax.axis_index("space")
    y_table = y_basis(grid_cols, ky_count)
    held_rows = (
        jnp.arange(space_count, dtype=jnp.int32)[:, None] * slab_rows
        + data_index * row_count
        + jnp.arange(row_count, dtype=jnp.int32)[None, :]
    ).reshape(held_count)
    x_held = x_rows_table(held_rows, grid_rows, kx_count)
    delta_field = (cotangent.astype(jnp.float32) * gelu_slope(pre_act.astype(jnp.float32))).astype(
        jnp.bfloat16
    )
    local_term = jnp.einsum(
        "bxyc,bxyo->co", field_in, delta_field, preferred_element_type=jnp.float32
    )
    bias_term = jnp.sum(delta_field, axis=(0, 1, 2), dtype=jnp.float32)
    local_sum, bias_sum = lax.psum((local_term, bias_term), ("dp", "space"))
    stacked = jnp.stack([field_in, delta_field])
    lines = lax.all_to_all(stacked, "dp", split_axis=2, concat_axis=3, tiled=True)
    pairs = lax.all_to_all(
        jnp.einsum("fbxyc,yr->fbxrc", lines, y_table, preferred_element_type=jnp.float32).astype(
            jnp.bfloat16
        ),
        "space",
        split_axis=3,
        concat_axis=2,
        tiled=True,
    )
    field_count = pairs.shape[0]
    split_pairs = pairs.reshape(field_count, batch_size, held_count, ky_local, 2, channels)
    table = x_held
    owned = lax.psum_scatter(
        jnp.einsum("qjpx,fbxkpc->jfbkqc", table, split_pairs, preferred_element_type=jnp.float32),
        "dp",
        scatter_dimension=0,
        tiled=True,
    ).astype(jnp.bfloat16)
    input_owned = owned[:, 0]
    delta_owned = owned[:, 1]
    ky_index = space_index * ky_local + jnp.arange(ky_local, dtype=jnp.int32)
    ky_scale = jnp.where(ky_index == 0, 1.0, 2.0).astype(jnp.float32) / (grid_rows * grid_cols)
    products = jnp.einsum(
        "jbkqc,jbkpo->jkqpco", input_owned, delta_owned, preferred_element_type=jnp.float32
    )
    grad_real = products[:, :, 0, 0] + products[:, :, 1, 1]
    grad_imag = products[:, :, 0, 1] - products[:, :, 1, 0]
    grad_spectral = (
        jnp.stack([grad_real, grad_imag], axis=2)
        * (ky_scale / batch_size)[None, :, None, None, None]
    ).astype(jnp.bfloat16)
    adjoint = jnp.einsum(
        "jbkpo,jkqco->bjkpqc", delta_owned, spec_weight, preferred_element_type=jnp.float32
    )
    back_real = adjoint[:, :, :, 0, 0] + adjoint[:, :, :, 1, 1]
    back_imag = adjoint[:, :, :, 1, 0] - adjoint[:, :, :, 0, 1]
    mode_back = (
        jnp.stack([back_real, back_imag], axis=3) * ky_scale[None, None, :, None, None]
    ).astype(jnp.bfloat16)
    table = x_held
    along_x = jnp.einsum(
        "qjpx,bjkqc->bxkpc",
        table,
        lax.all_gather(mode_back, "dp", axis=1, tiled=True),
        preferred_element_type=jnp.float32,
    ).astype(jnp.bfloat16)
    along_x = along_x.reshape(batch_size, held_count, 2 * ky_local, channels)
    lines_back = lax.all_to_all(along_x, "space", split_axis=1, concat_axis=2, tiled=True)
    local_part = jnp.einsum(
        "bxyo,co->bxyc", delta_field, local_weight, preferred_element_type=jnp.float32
    )
    slab_lines = lax.all_gather(lines_back, "dp", axis=1, tiled=True)
    y_block = lax.dynamic_slice_in_dim(y_table, data_index * col_block, col_block, 0)
    spectral_part = jnp.einsum(
        "bxrc,yr->bxyc", slab_lines, y_block, preferred_element_type=jnp.float32
    ).astype(jnp.bfloat16)
    grad_input = (spectral_part.astype(jnp.float32) + local_part).astype(jnp.bfloat16)
    return (grad_input, grad_spectral, local_sum / batch_size, bias_sum / batch_size)


def solution(mesh):
    placed = (
        P(None, "space", "dp", None),
        P(None, "space", "dp", None),
        P(None, "space", "dp", None),
        P("dp", "space", None, None, None),
        P(),
    )
    return jax.shard_map(
        on_device,
        mesh=mesh,
        in_specs=placed,
        out_specs=(P(None, "space", "dp", None), P("dp", "space", None, None, None), P(), P()),
        check_vma=False,
    )
```

profile of v0, /device:TPU:16, one launch (start us, length us, event | category | flops | bytes accessed | tf_op | source)
XLA Modules:
  0.0 838.3 jit_solution(12355432250104961929)
XLA Ops:
  8.0 1.2 convert_reduce_fusion
  9.3 1.6 pad_maximum_fusion
  10.9 14.8 %all-to-all-start = ((bf16[2,1,64,8,128]{4,3,1,0,2:T(8,128)(2,1)}), bf16[2,1,64,8,128]{4,3,1,0,2:T(8,128)(2,1)S(1)}, u32[]{:S(2)}, u32[]{:S(2)}) async-start(bf16[2,1,64,8,128]{4,3,1,0,2:T(8,128)(2,1)} %pad_maximum_fusion), calls=%async_computation | async-start | bytes 524288 | tf_op jit(solution)/shard_map/all_to_all | solution.py:71
  25.7 0.5 sine_negate_fusion
  26.5 12.6 %all-to-all-done = bf16[2,1,64,8,128]{4,3,1,0,2:T(8,128)(2,1)S(1)} async-done(((bf16[2,1,64,8,128]{4,3,1,0,2:T(8,128)(2,1)}), bf16[2,1,64,8,128]{4,3,1,0,2:T(8,128)(2,1)S(1)}, u32[]{:S(2)}, u32[]{:S(2)}) %all-to-all-start) | async-done | bytes 262176 | tf_op jit(solution)/shard_map/all_to_all | solution.py:71
  39.3 0.7 copy.85
  40.0 6.5 all-to-all-start.1
  46.7 5.5 all-to-all-done.1
  52.6 1.6 copy.88
  54.2 311.5 %reduce-scatter.2.cloned.1.call-done = f32[1,2,1,8,2,128]{5,3,4,2,1,0:T(8,128)} async-done(((f32[64,2,1,8,2,128]{5,3,4,2,1,0:T(8,128)}), f32[1,2,1,8,2,128]{5,3,4,2,1,0:T(8,128)}) %reduce-scatter.2.cloned.1.call-update) | async-done | bytes 16400 | tf_op jit(solution)/shard_map/reduce_scatter | solution.py:84
  365.7 0.7 convert_element_type.130
  366.8 152.5 %all_gather.6 = bf16[1,64,8,2,128]{4,2,3,0,1:T(8,128)(2,1)S(1)} all-gather(bf16[1,1,8,2,128]{4,2,3,0,1:T(8,128)(2,1)S(1)} %fusion.55), channel_id=1, replica_groups=mesh['dp'=64,'space'=8] {'dp'}, dimensions={1}, use_global_device_ids=true | all-gather | bytes 266240 | tf_op jit(solution)/shard_map/all_gather | solution.py:115
  519.5 0.6 copy.95
  520.1 6.3 all-to-all-start.2
  526.4 0.9 convolution_bitcast_fusion.2
  527.3 4.5 all-to-all-done.2
  531.9 0.6 copy-done.1
  532.6 96.2 %psum.15 = f32[128]{0:T(128)} all-reduce(f32[128]{0:T(128)S(1)} %get-tuple-element.28), channel_id=1, replica_groups=mesh['dp'=64,'space'=8] {'dp','space'}, use_global_device_ids=true, to_apply=%region_3.4 | all-reduce | flops 128 | bytes 1024 | tf_op jit(solution)/shard_map/psum | solution.py:69
  628.8 162.3 %all-reduce.2.cloned.1.call-done = f32[128,128]{0,1:T(8,128)} async-done(((f32[128,128]{0,1:T(8,128)}), f32[128,128]{0,1:T(8,128)}) %all-reduce.2.cloned.1.call-update) | async-done | bytes 65552 | tf_op jit(solution)/shard_map/psum | solution.py:69
  791.1 1.6 copy.98
  793.2 1.0 fusion.18
  794.2 33.7 %all-gather.2.cloned.1.call-done = bf16[1,64,128,128]{3,2,0,1:T(8,128)(2,1)} async-done(((bf16[1,1,128,128]{3,2,0,1:T(8,128)(2,1)}), bf16[1,64,128,128]{3,2,0,1:T(8,128)(2,1)}) %all-gather.2.cloned.1.call-update) | async-done | bytes 2097168 | tf_op jit(solution)/shard_map/all_gather | solution.py:123
  827.9 2.1 fusion.13
  830.0 0.9 fusion.3
  (32 shorter events, 2.1 us)
Async XLA Ops:
  8.0 358.4 %copy-start = (bf16[1,8,2,128,128]{4,3,2,1,0:T(8,128)(2,1)S(1)}, bf16[1,8,2,128,128]{4,3,2,1,0:T(8,128)(2,1)}, u32[]{:S(2)}) copy-start(bf16[1,8,2,128,128]{4,3,2,1,0:T(8,128)(2,1)} %param.8) | copy-start | bytes 1572868
  10.9 28.2 %all-to-all-start = ((bf16[2,1,64,8,128]{4,3,1,0,2:T(8,128)(2,1)}), bf16[2,1,64,8,128]{4,3,1,0,2:T(8,128)(2,1)S(1)}, u32[]{:S(2)}, u32[]{:S(2)}) async-start(bf16[2,1,64,8,128]{4,3,1,0,2:T(8,128)(2,1)} %pad_maximum_fusion), calls=%async_computation | async-start | bytes 524288 | tf_op jit(solution)/shard_map/all_to_all | solution.py:71
  40.0 12.2 %all-to-all-start.1 = ((bf16[2,1,1,128,128]{4,0,2,1,3:T(2,128)(2,1)}), bf16[2,1,1,128,128]{4,0,2,1,3:T(2,128)(2,1)S(1)}, u32[]{:S(2)}, u32[]{:S(2)}) async-start(bf16[2,1,1,128,128]{4,0,2,1,3:T(2,128)(2,1)} %copy.85), calls=%async_computation.1 | async-start | bytes 131072 | tf_op jit(solution)/shard_map/all_to_all | solution.py:72
  46.6 319.1 %reduce-scatter.2.cloned.1.call-start = ((), (), s32[]{:S(2)}) async-start(), calls=%async_computation.4 | async-start | bytes 1064960 | tf_op jit(solution)/shard_map/reduce_scatter | solution.py:84
  52.6 473.8 %copy-start.2 = (bf16[1,64,8,128]{3,2,1,0:T(8,128)(2,1)S(1)}, bf16[1,64,8,128]{3,2,1,0:T(8,128)(2,1)}, u32[]{:S(2)}) copy-start(bf16[1,64,8,128]{3,2,1,0:T(8,128)(2,1)} %param.5) | copy-start | bytes 393220
  520.1 11.8 %all-to-all-start.2 = ((bf16[1,8,16,128]{3,2,0,1:T(8,128)(2,1)}), bf16[1,8,16,128]{3,2,0,1:T(8,128)(2,1)S(1)}, u32[]{:S(2)}, u32[]{:S(2)}) async-start(bf16[1,8,16,128]{3,2,0,1:T(8,128)(2,1)} %copy.95), calls=%async_computation.3 | async-start | bytes 65536 | tf_op jit(solution)/shard_map/all_to_all | solution.py:119
  526.4 264.7 %all-reduce.2.cloned.1.call-start = ((), (), s32[]{:S(2)}) async-start(), calls=%async_computation.6 | async-start | bytes 131072 | tf_op jit(solution)/shard_map/psum | solution.py:69
  527.3 300.6 %all-gather.2.cloned.1.call-start = ((), (), s32[]{:S(2)}) async-start(), calls=%async_computation.5 | async-start | bytes 2129920 | tf_op jit(solution)/shard_map/all_gather | solution.py:123
  531.9 0.6 copy-start.1
  793.2 36.8 %copy-start.3 = (bf16[128,128]{1,0:T(8,128)(2,1)S(1)}, bf16[128,128]{1,0:T(8,128)(2,1)}, u32[]{:S(2)}) copy-start(bf16[128,128]{1,0:T(8,128)(2,1)} %param.9) | copy-start | bytes 98308
Sparse Core Ops, SparseCore 0:
  54.4 311.3 reduce-scatter.1
  532.6 295.2 all-gather.1
Sparse Core Ops, SparseCore 1:
  533.2 257.9 all-reduce.1
where the time goes:
time: 839 us; the launch traced here: 838 us
  waiting for transfers between devices  530 us (63%)
  blocking collectives  249 us (30%)
  starting transfers between devices  27.7 us (3%)
  between operations  15.6 us (2%)
    reduce_scatter x1, waiting for transfers between devices, on_device(): lax.psum_scatter(jnp.einsum('qjpx,fbxkpc->jfbkqc', table, split_pairs, pr...  311 us
    psum x1, waiting for transfers between devices, on_device(): local_sum, bias_sum = lax.psum((local_term, bias_term), ('dp', 'space'))  162 us
    all_gather x1, blocking collectives, on_device(): lax.all_gather(mode_back, 'dp', axis=1, tiled=True)  152 us
    psum x1, blocking collectives, on_device(): local_sum, bias_sum = lax.psum((local_term, bias_term), ('dp', 'space'))  96.2 us
    all_gather x1, waiting for transfers between devices, on_device(): slab_lines = lax.all_gather(lines_back, 'dp', axis=1, tiled=True)  33.7 us
  transfers between devices with their start and end apart: 6, of which 6 were waited for; matrix products, arithmetic and copies ran while one was open for 1% of the time, Pallas kernels for 0%

commit v1 on v0

--- a/solution.py
+++ b/solution.py
@@ -6,6 +6,13 @@
 
 root_two_pi = 0.7978845608028654
 cubic_coef = 0.044715
+
+
+def all_by_exchange(array, name, dim):
+    size = lax.axis_size(name)
+    blocks = jnp.stack([array for _ in range(size)])
+    blocks = lax.all_to_all(blocks, name, split_axis=0, concat_axis=0)
+    return jnp.concatenate(blocks, axis=dim)
 
 
 def gelu_slope(values):
@@ -112,7 +119,7 @@
     along_x = jnp.einsum(
         "qjpx,bjkqc->bxkpc",
         table,
-        lax.all_gather(mode_back, "dp", axis=1, tiled=True),
+        all_by_exchange(mode_back, "dp", 1),
         preferred_element_type=jnp.float32,
     ).astype(jnp.bfloat16)
     along_x = along_x.reshape(batch_size, held_count, 2 * ky_local, channels)

time: 839 us -> 703 us (0.84)
  blocking collectives: 249 us -> 111 us
    all_gather x1 -> x0, blocking collectives: 152 us -> none  [on_device(): lax.all_gather(mode_back, 'dp', axis=1, tiled=True)]
    all_to_all x0 -> x1, blocking collectives: none -> 15.9 us  [all_by_exchange(): blocks = lax.all_to_all(blocks, name, split_axis=0, concat_axis=0)]
where the time goes in v1:
time: 703 us; the launch traced here: 702 us
  waiting for transfers between devices  532 us (76%)
  blocking collectives  111 us (16%)
  starting transfers between devices  27.7 us (4%)
  between operations  15.6 us (2%)
    reduce_scatter x1, waiting for transfers between devices, on_device(): lax.psum_scatter(jnp.einsum('qjpx,fbxkpc->jfbkqc', table, split_pairs, pr...  311 us
    psum x1, waiting for transfers between devices, on_device(): local_sum, bias_sum = lax.psum((local_term, bias_term), ('dp', 'space'))  164 us
    psum x1, blocking collectives, on_device(): local_sum, bias_sum = lax.psum((local_term, bias_term), ('dp', 'space'))  95.4 us
    all_gather x1, waiting for transfers between devices, on_device(): slab_lines = lax.all_gather(lines_back, 'dp', axis=1, tiled=True)  33.7 us
    all_to_all x1, blocking collectives, all_by_exchange(): blocks = lax.all_to_all(blocks, name, split_axis=0, concat_axis=0)  15.9 us
    all_to_all x1, starting transfers between devices, on_device(): lax.all_to_all(stacked, 'dp', split_axis=2, concat_axis=3, tiled=True)  14.8 us
  transfers between devices with their start and end apart: 6, of which 6 were waited for; matrix products, arithmetic and copies ran while one was open for 1% of the time, Pallas kernels for 0%

profile of v1, /device:TPU:16, one launch (start us, length us, event | category | flops | bytes accessed | tf_op | source)
XLA Modules:
  0.0 702.5 jit_solution(92217505039615164)
XLA Ops:
  8.0 1.2 convert_reduce_fusion
  9.3 1.6 pad_maximum_fusion
  10.9 14.8 %all-to-all-start = ((bf16[2,1,64,8,128]{4,3,1,0,2:T(8,128)(2,1)}), bf16[2,1,64,8,128]{4,3,1,0,2:T(8,128)(2,1)S(1)}, u32[]{:S(2)}, u32[]{:S(2)}) async-start(bf16[2,1,64,8,128]{4,3,1,0,2:T(8,128)(2,1)} %pad_maximum_fusion), calls=%async_computation | async-start | bytes 524288 | tf_op jit(solution)/shard_map/all_to_all | solution.py:78
  25.7 0.5 sine_negate_fusion
  26.5 12.6 %all-to-all-done = bf16[2,1,64,8,128]{4,3,1,0,2:T(8,128)(2,1)S(1)} async-done(((bf16[2,1,64,8,128]{4,3,1,0,2:T(8,128)(2,1)}), bf16[2,1,64,8,128]{4,3,1,0,2:T(8,128)(2,1)S(1)}, u32[]{:S(2)}, u32[]{:S(2)}) %all-to-all-start) | async-done | bytes 262176 | tf_op jit(solution)/shard_map/all_to_all | solution.py:78
  39.3 0.7 copy.85
  40.0 6.5 all-to-all-start.1
  46.7 5.5 all-to-all-done.1
  52.6 1.6 copy.88
  54.2 311.5 %reduce-scatter.2.cloned.1.call-done = f32[1,2,1,8,2,128]{5,3,4,2,1,0:T(8,128)} async-done(((f32[64,2,1,8,2,128]{5,3,4,2,1,0:T(8,128)}), f32[1,2,1,8,2,128]{5,3,4,2,1,0:T(8,128)}) %reduce-scatter.2.cloned.1.call-update) | async-done | bytes 16400 | tf_op jit(solution)/shard_map/reduce_scatter | solution.py:91
  365.7 0.7 convert_element_type.129
  366.9 15.9 %all_to_all.35 = bf16[64,1,1,8,2,128]{5,4,3,2,1,0:T(2,128)(2,1)S(1)} all-to-all(bf16[64,1,1,8,2,128]{5,4,3,2,1,0:T(2,128)(2,1)S(1)} %stack.43), channel_id=1, replica_groups=mesh['dp'=64,'space'=8] {'dp'}, dimensions={0} | all-to-all | bytes 524288 | tf_op jit(solution)/shard_map/all_to_all | solution.py:14
  383.0 0.6 copy.95
  383.6 6.4 all-to-all-start.3
  390.0 0.9 convolution_bitcast_fusion.2
  390.9 4.6 all-to-all-done.3
  395.5 0.6 copy-done.1
  396.2 95.4 %psum.15 = f32[128]{0:T(128)} all-reduce(f32[128]{0:T(128)S(1)} %get-tuple-element.28), channel_id=1, replica_groups=mesh['dp'=64,'space'=8] {'dp','space'}, use_global_device_ids=true, to_apply=%region_3.4 | all-reduce | flops 128 | bytes 1024 | tf_op jit(solution)/shard_map/psum | solution.py:76
  491.6 163.8 %all-reduce.2.cloned.1.call-done = f32[128,128]{0,1:T(8,128)} async-done(((f32[128,128]{0,1:T(8,128)}), f32[128,128]{0,1:T(8,128)}) %all-reduce.2.cloned.1.call-update) | async-done | bytes 65552 | tf_op jit(solution)/shard_map/psum | solution.py:76
  655.3 1.6 copy.98
  657.4 1.0 fusion.18
  658.4 33.7 %all-gather.2.cloned.1.call-done = bf16[1,64,128,128]{3,2,0,1:T(8,128)(2,1)} async-done(((bf16[1,1,128,128]{3,2,0,1:T(8,128)(2,1)}), bf16[1,64,128,128]{3,2,0,1:T(8,128)(2,1)}) %all-gather.2.cloned.1.call-update) | async-done | bytes 2097168 | tf_op jit(solution)/shard_map/all_gather | solution.py:130
  692.1 2.1 fusion.13
  694.2 0.9 fusion.3
  (34 shorter events, 2.2 us)
Async XLA Ops:
  8.0 358.4 %copy-start = (bf16[1,8,2,128,128]{4,3,2,1,0:T(8,128)(2,1)S(1)}, bf16[1,8,2,128,128]{4,3,2,1,0:T(8,128)(2,1)}, u32[]{:S(2)}) copy-start(bf16[1,8,2,128,128]{4,3,2,1,0:T(8,128)(2,1)} %param.8) | copy-start | bytes 1572868
  10.9 28.2 %all-to-all-start = ((bf16[2,1,64,8,128]{4,3,1,0,2:T(8,128)(2,1)}), bf16[2,1,64,8,128]{4,3,1,0,2:T(8,128)(2,1)S(1)}, u32[]{:S(2)}, u32[]{:S(2)}) async-start(bf16[2,1,64,8,128]{4,3,1,0,2:T(8,128)(2,1)} %pad_maximum_fusion), calls=%async_computation | async-start | bytes 524288 | tf_op jit(solution)/shard_map/all_to_all | solution.py:78
  40.0 12.2 %all-to-all-start.1 = ((bf16[2,1,1,128,128]{4,0,2,1,3:T(2,128)(2,1)}), bf16[2,1,1,128,128]{4,0,2,1,3:T(2,128)(2,1)S(1)}, u32[]{:S(2)}, u32[]{:S(2)}) async-start(bf16[2,1,1,128,128]{4,0,2,1,3:T(2,128)(2,1)} %copy.85), calls=%async_computation.1 | async-start | bytes 131072 | tf_op jit(solution)/shard_map/all_to_all | solution.py:79
  46.6 319.1 %reduce-scatter.2.cloned.1.call-start = ((), (), s32[]{:S(2)}) async-start(), calls=%async_computation.5 | async-start | bytes 1064960 | tf_op jit(solution)/shard_map/reduce_scatter | solution.py:91
  52.6 337.4 %copy-start.2 = (bf16[1,64,8,128]{3,2,1,0:T(8,128)(2,1)S(1)}, bf16[1,64,8,128]{3,2,1,0:T(8,128)(2,1)}, u32[]{:S(2)}) copy-start(bf16[1,64,8,128]{3,2,1,0:T(8,128)(2,1)} %param.5) | copy-start | bytes 393220
  383.6 11.9 %all-to-all-start.3 = ((bf16[1,8,16,128]{3,2,0,1:T(8,128)(2,1)}), bf16[1,8,16,128]{3,2,0,1:T(8,128)(2,1)S(1)}, u32[]{:S(2)}, u32[]{:S(2)}) async-start(bf16[1,8,16,128]{3,2,0,1:T(8,128)(2,1)} %copy.95), calls=%async_computation.4 | async-start | bytes 65536 | tf_op jit(solution)/shard_map/all_to_all | solution.py:126
  390.0 265.3 %all-reduce.2.cloned.1.call-start = ((), (), s32[]{:S(2)}) async-start(), calls=%async_computation.7 | async-start | bytes 131072 | tf_op jit(solution)/shard_map/psum | solution.py:76
  390.9 301.2 %all-gather.2.cloned.1.call-start = ((), (), s32[]{:S(2)}) async-start(), calls=%async_computation.6 | async-start | bytes 2129920 | tf_op jit(solution)/shard_map/all_gather | solution.py:130
  395.5 0.6 copy-start.1
  657.4 36.8 %copy-start.3 = (bf16[128,128]{1,0:T(8,128)(2,1)S(1)}, bf16[128,128]{1,0:T(8,128)(2,1)}, u32[]{:S(2)}) copy-start(bf16[128,128]{1,0:T(8,128)(2,1)} %param.9) | copy-start | bytes 98308
Sparse Core Ops, SparseCore 0:
  54.4 311.3 reduce-scatter.1
  396.3 295.7 all-gather.1
Sparse Core Ops, SparseCore 1:
  396.8 258.5 all-reduce.1
